TPU v7x, 32 devices: a whole 2x2x4 slice. The times are simulated.
32 devices in a mesh: context: 4 (over y, x), expert: 8 (over z, core).
Axes of the slice: x: 2, y: 2, z: 4, core: 2. Of those that a mesh axis runs over, the one named last changes fastest.
Arguments:
- queries: bfloat16 [64, 3072], P(None, 'expert'), may hold values from -14 to 14
- key_lift: bfloat16 [16, 128, 512], P('expert'), may hold values from -0.5 to 0.5
- value_lift: bfloat16 [16, 512, 128], P('expert'), may hold values from -0.25 to 0.25
- page_pool: bfloat16 [16, 64, 576], P('context'), may hold values from -6 to 6
- fresh_latents: bfloat16 [8, 8, 576], P('context'), may hold values from -6 to 6
- page_table: int32 [8, 12], replicated, may hold values from 0 to 15, as said below
- context_lengths: int32 [8], replicated, may hold values from 705 to 768, as said below
- tree_parents: int32 [8, 8], replicated, may hold values from -1 to 6, as said below
- out_weight: bfloat16 [2048, 7168], P('expert', 'context'), may hold values from -0.5 to 0.5
- residual: bfloat16 [64, 7168], P('expert', 'context'), may hold values from -6 to 6
- norm_gain: float32 [7168], replicated, may hold values from 0.5 to 2
- expert_ids: int32 [64, 8], P('expert'), may hold values from 0 to 7, all different within a row; in each aligned block of 8 rows (0 to 7, 8 to 15, ...) at most 8 rows name the same one
- route_weights: float32 [64, 8], P('expert'), may hold values from 0.1 to 0.6
- gate_matrix: bfloat16 [8, 7168, 1024], P('expert', None, 'context'), may hold values from -0.0625 to 0.0625
- up_matrix: bfloat16 [8, 7168, 1024], P('expert', None, 'context'), may hold values from -0.0625 to 0.0625
- down_matrix: bfloat16 [8, 1024, 7168], P('expert', 'context'), may hold values from -0.1875 to 0.1875
Outputs:
- layer_out: bfloat16 [64, 7168], P('expert', 'context')
Inputs may be any that keep to these rules, and one draw needn't show every extreme that they name: `page_table`: the 12 pages of a leaf are distinct. `context_lengths`: entry k of a leaf's page table holds its context tokens k * 64 to k * 64 + 63; some leaf fills all 12 pages. `tree_parents`: token 0 of a leaf has parent -1; token t > 0 has a parent among tokens 0 to t - 1 of the same leaf. `expert_ids`: within each aligned block of 8 rows, no expert is named by more than 8 rows, a bound that some block reaches.
All inputs are finite; a program needn't handle non-finite values.
Results may differ from a plain program's by a relative error of at most 0.011.
Values may be sent and summed in bfloat16 or wider, within the bound.
A program may use at most 64 MiB of HBM per device.

v0:
```python
import functools

import jax
import jax.numpy as jnp
from jax import lax
from jax.experimental import pallas as pl
from jax.experimental.pallas import tpu as pltpu
from jax.sharding import PartitionSpec as P

LAT = 512
ROPE = 64
QK = 128
VD = 128
NEG = -(2.0**100)
EPS = 1e-06
F32 = jnp.float32
BF16 = jnp.bfloat16
MESH = pl.DeviceIdType.MESH
STAT = 128


def iota(shape, dim):
    return lax.broadcasted_iota(jnp.int32, shape, dim)


def dot(a, b):
    return jnp.dot(a, b, preferred_element_type=F32)


def dot_t(a, b):
    return lax.dot_general(a, b, (((1,), (1,)), ((), ())), preferred_element_type=F32)


def div(v, n):
    return jnp.right_shift(v, n.bit_length() - 1) if n & (n - 1) == 0 else v // n


def mod(v, n):
    return v & (n - 1) if n & (n - 1) == 0 else v % n


def spread(per_leaf, advance):
    leaves, n = per_leaf.shape
    return jnp.broadcast_to(per_leaf[:, None, :], (leaves, advance, n)).reshape(leaves * advance, n)


def masks(c, pt_ref, cl_ref, tp_ref, pool_keys, page_len, fresh_cols, own_leaves):
    leaves, slots = pt_ref.shape
    advance = tp_ref.shape[1]
    rows = leaves * advance
    lengths = jnp.sum(
        jnp.where(
            iota((leaves, leaves), 0) == iota((leaves, leaves), 1),
            jnp.broadcast_to(cl_ref[...].astype(F32), (leaves, leaves)),
            0.0,
        ),
        axis=1,
        keepdims=True,
    )
    remain = lengths - (iota((leaves, slots), 1) * page_len).astype(F32)
    table = pt_ref[...]
    lane = iota((leaves, pool_keys), 1)
    limit = jnp.zeros((leaves, pool_keys), F32)
    pages = pool_keys // page_len
    for p in range(pages):
        here = jnp.sum(jnp.where(table == c * pages + p, remain, 0.0), axis=1, keepdims=True)
        limit = jnp.where(div(lane, page_len) == p, here, limit)
    inside = jnp.where(mod(lane, page_len).astype(F32) < limit, 1.0, 0.0)
    pool_mask = spread(inside, advance)
    token = mod(iota((leaves, fresh_cols), 1), advance)
    parents = tp_ref[...]
    chains = [jnp.where(token == 0, 1.0, 0.0)]
    for t in range(1, advance):
        chain = jnp.where(token == t, 1.0, 0.0)
        for u in range(t):
            chain = jnp.where(parents[:, t : t + 1] == u, chain + chains[u], chain)
        chains.append(chain)
    row = iota((rows, fresh_cols), 0)
    col = iota((rows, fresh_cols), 1)
    linked = jnp.zeros((rows, fresh_cols), F32)
    for t in range(advance):
        linked = jnp.where(mod(row, advance) == t, spread(chains[t], advance), linked)
    own = (div(row, advance) == c * own_leaves + div(col, advance)) & (col < own_leaves * advance)
    fresh_mask = jnp.where(own, linked, 0.0)
    return jnp.concatenate([pool_mask, fresh_mask], axis=1) > 0.5


def kernel(
    nctx, nexp, page_len, own_leaves,
    q_hbm, kl_hbm, vl_hbm, pool_hbm, fresh_hbm, pt_hbm, cl_hbm, tp_hbm, ow_hbm, res_ref, gain_hbm, ids_hbm,
    rw_hbm, g_hbm, u_hbm, d_hbm, out_ref,
    q_ref, kl_ref, vl_ref, pt_ref, cl_ref, tp_ref, gain_ref, ids_ref, rw_ref,
    kf, att_send, att_recv, w2, g_v, u_v, d_v, w_all, zf, zs, zr, xg, pf, ps, pr, cs, cr, yf, ys, yr,
    loc, att_ss, att_rs, w2_ss, w2_rs, w_ss, w_rs, wp_ss, wp_rs, z_ss, z_rs, agz_ss, agz_rs, agc_ss, agc_rs,
    agp_ss, agp_rs, p_ss, p_rs, c_ss, c_rs, y_ss, y_rs,
):
    c = lax.axis_index("context")
    e = lax.axis_index("expert")
    k, z = e % 2, e // 2
    nz = nexp // 2
    rows = q_hbm.shape[0]
    half_rows = rows // 2
    heads = kl_hbm.shape[0]
    row_dev, cols = res_ref.shape
    half = cols // 2
    other = 1 - k

    near = [((c // 2 + d // 2) % (nctx // 2)) * 2 + (c + d) % 2 for d in range(nctx)]
    turn = 1 - 2 * (z // (nz // 2))

    def ctx(d):
        return near[d]

    def zat(d):
        return (z + turn * d + nz) % nz

    def dev(cc, zz, kk):
        return (cc, zz * 2 + kk)

    def send(src, dst, ss, rs, to):
        return pltpu.make_async_remote_copy(
            src_ref=src, dst_ref=dst, send_sem=ss, recv_sem=rs, device_id=to, device_id_type=MESH
        )

    def got(dst, ss, rs):
        send(dst, dst, ss, rs, dev(c, z, other)).wait_recv()

    def z_loop(body):
        lax.fori_loop(1, nz, lambda d, carry: (body(zat(d)), carry)[1], 0)

    barrier = pltpu.get_barrier_semaphore()
    for d in range(nctx):
        for kk in range(2):
            if d or kk:
                pl.semaphore_signal(
                    barrier, inc=1, device_id=dev(ctx(d), z, (k + kk) % 2), device_id_type=MESH
                )
    z_loop(lambda zp: pl.semaphore_signal(barrier, inc=1, device_id=dev(c, zp, k), device_id_type=MESH))

    pool_keys = pool_hbm.shape[0]
    fresh_keys = fresh_hbm.shape[0]
    fresh_cols = kf.shape[0] - pool_keys
    pairs = [
        (pt_hbm, pt_ref),
        (cl_hbm, cl_ref),
        (tp_hbm, tp_ref),
        (ids_hbm, ids_ref),
        (rw_hbm, rw_ref),
        (q_hbm, q_ref),
        (kl_hbm, kl_ref),
        (pool_hbm, kf.at[0:pool_keys, :]),
        (fresh_hbm, kf.at[pool_keys : pool_keys + fresh_keys, :]),
        (vl_hbm, vl_ref),
        (ow_hbm, w2.at[k]),
        (gain_hbm, gain_ref),
        (g_hbm, g_v),
        (u_hbm, u_v),
        (d_hbm, d_v),
    ]
    local = [pltpu.make_async_copy(src, dst, loc.at[i]) for i, (src, dst) in enumerate(pairs)]
    for copy in local:
        copy.start()
    if fresh_cols != fresh_keys:
        kf[pool_keys + fresh_keys :, :] = jnp.zeros((fresh_cols - fresh_keys, kf.shape[1]), BF16)
    for copy in local[:5]:
        copy.wait()

    lane_w = iota((row_dev, STAT), 1)
    dense = jnp.zeros((row_dev, STAT), F32)
    ids, rw = ids_ref[...], rw_ref[...]
    for t in range(ids.shape[1]):
        dense = jnp.where(lane_w == ids[:, t : t + 1], rw[:, t : t + 1], dense)
    w_all[k, z] = dense

    mask = masks(c, pt_ref, cl_ref, tp_ref, pool_keys, page_len, fresh_cols, own_leaves)
    for copy in local[5:9]:
        copy.wait()
    qf = q_ref[...].astype(F32)
    scale = (QK + ROPE) ** (-0.5)
    keys = kf[...]
    lat, rot = [], []
    for h in range(heads):
        at = h * (QK + ROPE)
        lat.append(dot(qf[:, at : at + QK].astype(BF16), kl_ref[h]).astype(BF16))
        rot.append(qf[:, at + QK : at + QK + ROPE].astype(BF16))
    scores = dot_t(jnp.concatenate(lat, axis=0), keys[:, :LAT])
    scores = (scores + dot_t(jnp.concatenate(rot, axis=0), keys[:, LAT:])) * scale
    scores = jnp.concatenate(
        [jnp.where(mask, scores[h * rows : (h + 1) * rows], NEG) for h in range(heads)], axis=0
    )
    top = jnp.max(scores, axis=1, keepdims=True).astype(BF16).astype(F32)
    weight = jnp.exp(scores - top)
    total = jnp.sum(weight, axis=1, keepdims=True)
    numer = dot(weight.astype(BF16), keys[:, :LAT]) / total
    local[9].wait()
    high = numer.astype(BF16)
    low = (numer - high.astype(F32)).astype(BF16)
    t_high = total.astype(BF16).astype(F32)
    parts = []
    lane_s = iota((rows, STAT), 1)
    stats = jnp.zeros((rows, STAT), F32)
    for h in range(heads):
        own = slice(h * rows, (h + 1) * rows)
        parts.append(dot(high[own], vl_ref[h]) + dot(low[own], vl_ref[h]))
        for i, value in enumerate((top, t_high, total - t_high)):
            stats = jnp.where(lane_s == 3 * h + i, value[own], stats)
    width = heads * VD + STAT
    message = jnp.concatenate(parts + [stats], axis=1).reshape(nz, 2, row_dev, width)
    for kk in range(2):
        att_send[kk] = message[:, kk].reshape(half_rows, width).astype(BF16)
    att_recv[c * 2 + k] = att_send[k]

    pl.semaphore_wait(barrier, 2 * nctx - 1 + nz - 1)
    att_copies = []
    for d in range(nctx - 1, -1, -1):
        for kk in range(2):
            if d or kk:
                to = (k + kk) % 2
                att_copies.append(
                    send(att_send.at[to], att_recv.at[c * 2 + k], att_ss.at[2 * d + kk], att_rs.at[c * 2 + k],
                         dev(ctx(d), z, to))
                )
                att_copies[-1].start()
    w2_copy = send(ow_hbm, w2.at[k], w2_ss, w2_rs, dev(c, z, other))
    w2_copy.start()
    z_loop(lambda zp: send(w_all.at[k, z], w_all.at[k, z], w_ss.at[zp], w_rs.at[z], dev(c, zp, k)).start())
    for d in range(nctx):
        for kk in range(2):
            if d or kk:
                slot = ctx(d) * 2 + (k + kk) % 2
                got(att_recv.at[slot], att_ss.at[0], att_rs.at[slot])

    merged = []
    for kk in range(2):
        held = [att_recv[cc * 2 + kk].astype(F32) for cc in range(nctx)]
        for h in range(heads):
            base = heads * VD + 3 * h
            tops = [v[:, base : base + 1] for v in held]
            best = functools.reduce(jnp.maximum, tops)
            shares = [
                (v[:, base + 1 : base + 2] + v[:, base + 2 : base + 3]) * jnp.exp(t - best)
                for v, t in zip(held, tops)
            ]
            whole = functools.reduce(jnp.add, shares)
            mixed = functools.reduce(
                jnp.add, [s * v[:, h * VD : (h + 1) * VD] for s, v in zip(shares, held)]
            )
            merged.append((mixed / whole).astype(BF16))
    local[10].wait()
    got(w2.at[other], w2_ss, w2_rs)
    span = heads
    projected = dot(jnp.concatenate(merged[:span], axis=1), w2[0]) + dot(
        jnp.concatenate(merged[span:], axis=1), w2[1]
    )

    def fold(v):
        v = v.reshape(-1, row_dev, cols)
        return jnp.concatenate([v[:, :, :half], v[:, :, half:]], axis=1)

    folded = fold(projected)
    zf[...] = folded
    zs[...] = folded.astype(BF16)
    z_loop(lambda zp: send(zs.at[zp], zr.at[z], z_ss.at[zp], z_rs.at[z], dev(c, zp, k)).start())
    state = zf[z] + fold(res_ref[...].astype(F32))[0]

    def take(d, acc):
        zp = zat(d)
        got(zr.at[zp], z_ss.at[zp], z_rs.at[zp])
        return acc + zr[zp].astype(F32)

    state = lax.fori_loop(1, nz, take, state)
    hidden = state.astype(BF16)
    xg[c, k, z] = hidden

    def ag_z(zp):
        return send(xg.at[c, k, z], xg.at[c, k, z], agz_ss.at[zp], agz_rs.at[z], dev(c, zp, k))

    def ag_c(d, zp):
        piece = xg.at[c, k, zp]
        return send(piece, piece, agc_ss.at[d, zp], agc_rs.at[c, zp], dev(ctx(d), z, k))

    def ag_p(cc, zp):
        piece = xg.at[cc, k, zp]
        return send(piece, piece, agp_ss.at[cc, zp], agp_rs.at[cc, zp], dev(c, z, other))

    z_loop(lambda zp: ag_z(zp).start())

    def onward(zp):
        for d in range(1, nctx - 1):
            ag_c(d, zp).start()
        ag_p(c, zp).start()

    def arrived(zp):
        got(xg.at[c, k, zp], agz_ss.at[zp], agz_rs.at[zp])
        onward(zp)

    onward(z)
    z_loop(arrived)
    ag_c(nctx - 1, z).start()
    z_loop(lambda zp: ag_c(nctx - 1, zp).start())

    def relay(d):
        def body(step, carry):
            zp = zat(step)
            got(xg.at[ctx(d), k, zp], agc_ss.at[0, zp], agc_rs.at[ctx(d), zp])
            ag_p(ctx(d), zp).start()
            return carry

        lax.fori_loop(0, nz, body, 0)

    z_loop(lambda zp: got(w_all.at[k, zp], w_ss.at[zp], w_rs.at[zp]))
    wp_copy = send(w_all.at[k], w_all.at[k], wp_ss, wp_rs, dev(c, z, other))
    wp_copy.start()

    for copy in local[11:14]:
        copy.wait()
    acc = [jnp.zeros((rows, 1), F32), jnp.zeros((rows, g_v.shape[1]), F32), jnp.zeros((rows, g_v.shape[1]), F32)]

    def expand(d):
        cc = ctx(d)

        def body(zp, carry):
            got(xg.at[cc, other, zp], agp_ss.at[cc, zp], agp_rs.at[cc, zp])
            return carry

        lax.fori_loop(0, nz, body, 0)
        both = [xg[cc, kk].astype(F32) for kk in (k, other)]
        for i in range(2):
            x = jnp.concatenate(
                [v[:, i * row_dev : (i + 1) * row_dev].reshape(half_rows, half) for v in both], axis=0
            )
            at = pl.ds(pl.multiple_of(cc * cols + i * half, half), half)
            scaled = (x * gain_ref[:, at]).astype(BF16)
            acc[0] = acc[0] + jnp.sum(x * x, axis=1, keepdims=True)
            acc[1] = acc[1] + dot(scaled, g_v[at, :])
            acc[2] = acc[2] + dot(scaled, u_v[at, :])

    relay(1)
    expand(0)
    for d in range(2, nctx):
        relay(d)
        expand(d - 1)
    expand(nctx - 1)

    inverse = lax.rsqrt(acc[0] * (1.0 / (nctx * cols)) + EPS)
    gate, up = acc[1] * inverse, acc[2] * inverse
    got(w_all.at[other], wp_ss, wp_rs)
    weights = jnp.concatenate(
        [w_all[kk].reshape(half_rows, STAT) for kk in (k, other)], axis=0
    )
    weight = jnp.sum(jnp.where(iota((rows, STAT), 1) == e, weights, 0.0), axis=1, keepdims=True)
    active = jnp.where(weight > 0.0, gate / (1.0 + jnp.exp(-gate)) * up, 0.0).astype(BF16)
    local[14].wait()

    def contract(d):
        at = pl.ds(pl.multiple_of(ctx(d) * cols, cols), cols)
        out = dot(active, d_v[:, at]) * weight
        pf[d] = out[:half_rows]
        ps[d] = out[half_rows:].astype(BF16)
        pair(d).start()

    def pair(d):
        return send(ps.at[d], pr.at[d], p_ss.at[d], p_rs.at[d], dev(c, z, other))

    def across(d):
        return send(cs.at[d], cr.at[c], c_ss.at[d], c_rs.at[c], dev(ctx(d), z, k))

    def join(d):
        got(pr.at[d], p_ss.at[d], p_rs.at[d])
        both = pf[d] + pr[d].astype(F32)
        if d:
            cs[d] = both.astype(BF16)
            across(d).start()
        return both

    order = list(range(nctx - 1, -1, -1))
    contract(order[0])
    for before, now in zip(order[:-1], order[1:]):
        contract(now)
        join(before)
    total = join(0)
    for d in range(1, nctx):
        cc = ctx(d)
        got(cr.at[cc], c_ss.at[d], c_rs.at[cc])
        total = total + cr[cc].astype(F32)

    folded = fold(total)
    yf[...] = folded
    ys[...] = folded.astype(BF16)

    def send_y(zp):
        return send(ys.at[zp], yr.at[z], y_ss.at[zp], y_rs.at[z], dev(c, zp, k))

    z_loop(lambda zp: send_y(zp).start())
    for copy in att_copies:
        copy.wait_send()
    w2_copy.wait_send()
    wp_copy.wait_send()

    def drain_z(zp):
        send(w_all.at[k, z], w_all.at[k, z], w_ss.at[zp], w_rs.at[z], dev(c, zp, k)).wait_send()
        send(zs.at[zp], zr.at[z], z_ss.at[zp], z_rs.at[z], dev(c, zp, k)).wait_send()
        ag_z(zp).wait_send()

    z_loop(drain_z)

    def drain(zp, carry):
        for d in range(nctx):
            if d:
                ag_c(d, zp).wait_send()
            ag_p(ctx(d), zp).wait_send()
        return carry

    lax.fori_loop(0, nz, drain, 0)
    for d in range(nctx):
        pair(d).wait_send()
        if d:
            across(d).wait_send()
    result = hidden.astype(F32) + yf[z]

    def take_last(d, acc):
        zp = zat(d)
        got(yr.at[zp], y_ss.at[zp], y_rs.at[zp])
        return acc + yr[zp].astype(F32)

    result = lax.fori_loop(1, nz, take_last, result)
    out_ref[...] = jnp.concatenate([result[:row_dev], result[row_dev:]], axis=1).astype(BF16)

    z_loop(lambda zp: send_y(zp).wait_send())


def local(
    nctx, nexp,
    queries, key_lift, value_lift, page_pool, fresh_latents, page_table, context_lengths, tree_parents,
    out_weight, residual, norm_gain, expert_ids, route_weights, gate_matrix, up_matrix, down_matrix,
):
    nz = nexp // 2
    rows = queries.shape[0]
    half_rows = rows // 2
    row_dev, cols = residual.shape
    half = cols // 2
    heads = key_lift.shape[0]
    width = heads * VD + STAT
    own_leaves, advance, ckv = fresh_latents.shape
    fresh_cols = -(-own_leaves * advance // 128) * 128
    gate, up, down = gate_matrix[0], up_matrix[0], down_matrix[0]
    lengths, gain = context_lengths.reshape(1, -1), norm_gain.reshape(1, -1)
    dma = pltpu.SemaphoreType.DMA
    vm = pl.BlockSpec(memory_space=pltpu.VMEM)
    hbm = pl.BlockSpec(memory_space=pl.ANY)
    piece = (2 * row_dev, half)
    scratch = [pltpu.VMEM(a.shape, a.dtype) for a in (
        queries, key_lift, value_lift, page_table, lengths, tree_parents, gain, expert_ids, route_weights
    )] + [
        pltpu.VMEM((page_pool.shape[0] * page_pool.shape[1] + fresh_cols, ckv), BF16),
        pltpu.VMEM((2, half_rows, width), BF16),
        pltpu.VMEM((2 * nctx, half_rows, width), BF16),
        pltpu.VMEM((2,) + out_weight.shape, BF16),
        pltpu.VMEM(gate.shape, BF16),
        pltpu.VMEM(up.shape, BF16),
        pltpu.VMEM(down.shape, BF16),
        pltpu.VMEM((2, nz, row_dev, STAT), F32),
        pltpu.VMEM((nz,) + piece, F32),
        pltpu.VMEM((nz,) + piece, BF16),
        pltpu.VMEM((nz,) + piece, BF16),
        pltpu.VMEM((nctx, 2, nz) + piece, BF16),
        pltpu.VMEM((nctx, half_rows, cols), F32),
        pltpu.VMEM((nctx, half_rows, cols), BF16),
        pltpu.VMEM((nctx, half_rows, cols), BF16),
        pltpu.VMEM((nctx, half_rows, cols), BF16),
        pltpu.VMEM((nctx, half_rows, cols), BF16),
        pltpu.VMEM((nz,) + piece, F32),
        pltpu.VMEM((nz,) + piece, BF16),
        pltpu.VMEM((nz,) + piece, BF16),
        dma((15,)),
        dma((2 * nctx,)), dma((2 * nctx,)),
        dma, dma,
        dma((nz,)), dma((nz,)),
        dma, dma,
        dma((nz,)), dma((nz,)),
        dma((nz,)), dma((nz,)),
        dma((nctx, nz)), dma((nctx, nz)),
        dma((nctx, nz)), dma((nctx, nz)),
        dma((nctx,)), dma((nctx,)),
        dma((nctx,)), dma((nctx,)),
        dma((nz,)), dma((nz,)),
    ]
    return pl.pallas_call(
        functools.partial(kernel, nctx, nexp, page_pool.shape[1], own_leaves),
        out_shape=jax.ShapeDtypeStruct((row_dev, cols), BF16),
        in_specs=[hbm] * 9 + [vm] + [hbm] * 6,
        out_specs=vm,
        scratch_shapes=scratch,
        compiler_params=pltpu.CompilerParams(
            collective_id=0, has_side_effects=True, vmem_limit_bytes=60 * 2**20
        ),
    )(
        queries, key_lift, value_lift, page_pool.reshape(-1, ckv), fresh_latents.reshape(-1, ckv), page_table,
        lengths, tree_parents, out_weight, residual, gain,
        expert_ids, route_weights, gate, up, down,
    )


def solution(mesh):
    return jax.shard_map(
        functools.partial(local, mesh.shape["context"], mesh.shape["expert"]),
        mesh=mesh,
        in_specs=(
            P(None, "expert"),
            P("expert", None, None),
            P("expert", None, None),
            P("context", None, None),
            P("context", None, None),
            P(),
            P(),
            P(),
            P("expert", "context"),
            P("expert", "context"),
            P(),
            P("expert", None),
            P("expert", None),
            P("expert", None, "context"),
            P("expert", None, "context"),
            P("expert", "context", None),
        ),
        out_specs=P("expert", "context"),
        check_vma=False,
    )
```

profile of v0, /device:TPU:0, one launch (start us, length us, event | category | flops | bytes accessed | tf_op | source)
XLA Modules:
  0.0 43.1 jit_solution(8180977314373624626)
XLA Ops:
  0.0 41.7 %shard_map.154 = bf16[8,1792]{1,0:T(8,128)(2,1)} custom-call(bf16[64,384]{1,0:T(8,128)(2,1)} %q_hbm.1, bf16[2,128,512]{2,1,0:T(8,128)(2,1)} %kl_hbm.1, bf16[2,512,128]{2,1,0:T(8,128)(2,1)} %vl_hbm.1, bf16[256,576]{1,0:T(8,128)(2,1)} %bitcast.10, bf16[16,576]{1,0:T(8,128)(2,1)} %bitcast.12, s32[8,12]{1,0:T(8,128)} %pt_hbm.1, s32[1,8]{1,0:T(1,128)} %bitcast.13, ...), custom_call_target="tpu_custom_call" | custom-call | tf_op jit(solution)/shard_map/pallas_call | solution.py:488
  41.7 1.4 %copy.18 = bf16[8,1792]{1,0:T(8,128)(2,1)} copy(bf16[8,1792]{1,0:T(8,128)(2,1)} %shard_map.154) | data formatting | bytes 57344
where the time goes:
time: 43.3 us; the launch traced here: 43.1 us
  Pallas kernels  41.7 us (96%)
  local copies, waits for them, and re-layouts  1.36 us (3%)
    pallas_call x1, Pallas kernels, local(): pl.pallas_call(functools.partial(kernel, nctx, nexp, page_pool.shape[1],...  41.7 us
    unnamed x1, local copies, waits for them, and re-layouts  1.36 us

commit v1 on v0

--- a/solution.py
+++ b/solution.py
@@ -90,9 +90,9 @@
     q_hbm, kl_hbm, vl_hbm, pool_hbm, fresh_hbm, pt_hbm, cl_hbm, tp_hbm, ow_hbm, res_ref, gain_hbm, ids_hbm,
     rw_hbm, g_hbm, u_hbm, d_hbm, out_ref,
     q_ref, kl_ref, vl_ref, pt_ref, cl_ref, tp_ref, gain_ref, ids_ref, rw_ref,
-    kf, att_send, att_recv, w2, g_v, u_v, d_v, w_all, zf, zs, zr, xg, pf, ps, pr, cs, cr, yf, ys, yr,
+    kf, att_send, att_recv, w2, g_v, u_v, d_v, w_all, zf, zs, zr, xg, pf, ps, pr, cs, cr, yf, ys, yr, vf, vs, vr, ts, tr,
     loc, att_ss, att_rs, w2_ss, w2_rs, w_ss, w_rs, wp_ss, wp_rs, z_ss, z_rs, agz_ss, agz_rs, agc_ss, agc_rs,
-    agp_ss, agp_rs, p_ss, p_rs, c_ss, c_rs, y_ss, y_rs,
+    agp_ss, agp_rs, p_ss, p_rs, c_ss, c_rs, y_ss, y_rs, v_ss, v_rs, t_ss, t_rs,
 ):
     c = lax.axis_index("context")
     e = lax.axis_index("expert")
@@ -158,7 +158,7 @@
         (d_hbm, d_v),
     ]
     local = [pltpu.make_async_copy(src, dst, loc.at[i]) for i, (src, dst) in enumerate(pairs)]
-    for copy in local:
+    for copy in local[:10]:
         copy.start()
     if fresh_cols != fresh_keys:
         kf[pool_keys + fresh_keys :, :] = jnp.zeros((fresh_cols - fresh_keys, kf.shape[1]), BF16)
@@ -173,8 +173,10 @@
     w_all[k, z] = dense
 
     mask = masks(c, pt_ref, cl_ref, tp_ref, pool_keys, page_len, fresh_cols, own_leaves)
-    for copy in local[5:9]:
+    for copy in local[5:10]:
         copy.wait()
+    for copy in local[10:]:
+        copy.start()
     qf = q_ref[...].astype(F32)
     scale = (QK + ROPE) ** (-0.5)
     keys = kf[...]
@@ -192,7 +194,6 @@
     weight = jnp.exp(scores - top)
     total = jnp.sum(weight, axis=1, keepdims=True)
     numer = dot(weight.astype(BF16), keys[:, :LAT]) / total
-    local[9].wait()
     high = numer.astype(BF16)
     low = (numer - high.astype(F32)).astype(BF16)
     t_high = total.astype(BF16).astype(F32)
@@ -253,15 +254,19 @@
         jnp.concatenate(merged[span:], axis=1), w2[1]
     )
 
-    def fold(v):
-        v = v.reshape(-1, row_dev, cols)
-        return jnp.concatenate([v[:, :, :half], v[:, :, half:]], axis=1)
-
-    folded = fold(projected)
+    def fold(v, count):
+        v = v.reshape(-1, count, v.shape[-1])
+        mid = v.shape[-1] // 2
+        return jnp.concatenate([v[:, :, :mid], v[:, :, mid:]], axis=1)
+
+    def unfold(v, count):
+        return jnp.concatenate([v[:count], v[count:]], axis=1)
+
+    folded = fold(projected, row_dev)
     zf[...] = folded
     zs[...] = folded.astype(BF16)
     z_loop(lambda zp: send(zs.at[zp], zr.at[z], z_ss.at[zp], z_rs.at[z], dev(c, zp, k)).start())
-    state = zf[z] + fold(res_ref[...].astype(F32))[0]
+    state = zf[z] + fold(res_ref[...].astype(F32), row_dev)[0]
 
     def take(d, acc):
         zp = zat(d)
@@ -369,10 +374,25 @@
         got(pr.at[d], p_ss.at[d], p_rs.at[d])
         both = pf[d] + pr[d].astype(F32)
         if d:
-            cs[d] = both.astype(BF16)
+            cs[d] = both[:, :wide].astype(BF16)
             across(d).start()
-        return both
-
+        side.append(both[:, wide:].reshape(nz, row_dev, cols - wide))
+        if len(side) % 2 == 0:
+            g = len(side) // 2 - 1
+            stack = jnp.concatenate(side[-2:], axis=1)
+            vf[g] = stack
+            vs[g] = stack.astype(BF16)
+            z_loop(lambda zp: send_v(g, zp).start())
+        return both[:, :wide]
+
+    def send_v(g, zp):
+        return send(vs.at[g, zp], vr.at[g, z], v_ss.at[g, zp], v_rs.at[g, z], dev(c, zp, k))
+
+    def send_t(d):
+        return send(ts.at[d], tr.at[c], t_ss.at[d], t_rs.at[c], dev(ctx(d), z, k))
+
+    wide = cs.shape[2]
+    side = []
     order = list(range(nctx - 1, -1, -1))
     contract(order[0])
     for before, now in zip(order[:-1], order[1:]):
@@ -384,7 +404,7 @@
         got(cr.at[cc], c_ss.at[d], c_rs.at[cc])
         total = total + cr[cc].astype(F32)
 
-    folded = fold(total)
+    folded = fold(total, row_dev)
     yf[...] = folded
     ys[...] = folded.astype(BF16)
 
@@ -392,6 +412,22 @@
         return send(ys.at[zp], yr.at[z], y_ss.at[zp], y_rs.at[z], dev(c, zp, k))
 
     z_loop(lambda zp: send_y(zp).start())
+
+    sides = [None] * nctx
+    for g in range(nctx // 2):
+
+        def take_v(d, acc, g=g):
+            zp = zat(d)
+            got(vr.at[g, zp], v_ss.at[g, zp], v_rs.at[g, zp])
+            return acc + vr[g, zp].astype(F32)
+
+        summed = lax.fori_loop(1, nz, take_v, vf[g, z])
+        for i in range(2):
+            d = order[2 * g + i]
+            sides[d] = summed[i * row_dev : (i + 1) * row_dev]
+            if d:
+                ts[d] = fold(sides[d], row_dev)[0].astype(BF16)
+                send_t(d).start()
     for copy in att_copies:
         copy.wait_send()
     w2_copy.wait_send()
@@ -401,6 +437,8 @@
         send(w_all.at[k, z], w_all.at[k, z], w_ss.at[zp], w_rs.at[z], dev(c, zp, k)).wait_send()
         send(zs.at[zp], zr.at[z], z_ss.at[zp], z_rs.at[z], dev(c, zp, k)).wait_send()
         ag_z(zp).wait_send()
+        for g in range(nctx // 2):
+            send_v(g, zp).wait_send()
 
     z_loop(drain_z)
 
@@ -416,16 +454,21 @@
         pair(d).wait_send()
         if d:
             across(d).wait_send()
-    result = hidden.astype(F32) + yf[z]
+    side_sum = sides[0]
+    for d in range(1, nctx):
+        got(tr.at[ctx(d)], t_ss.at[d], t_rs.at[ctx(d)])
+        side_sum = side_sum + unfold(tr[ctx(d)].astype(F32), row_dev)
 
     def take_last(d, acc):
         zp = zat(d)
         got(yr.at[zp], y_ss.at[zp], y_rs.at[zp])
         return acc + yr[zp].astype(F32)
 
-    result = lax.fori_loop(1, nz, take_last, result)
-    out_ref[...] = jnp.concatenate([result[:row_dev], result[row_dev:]], axis=1).astype(BF16)
-
+    main_sum = unfold(lax.fori_loop(1, nz, take_last, yf[z]), row_dev)
+    result = unfold(hidden.astype(F32), row_dev) + jnp.concatenate([main_sum, side_sum], axis=1)
+    out_ref[...] = result.astype(BF16)
+    for d in range(1, nctx):
+        send_t(d).wait_send()
     z_loop(lambda zp: send_y(zp).wait_send())
 
 
@@ -449,6 +492,8 @@
     vm = pl.BlockSpec(memory_space=pltpu.VMEM)
     hbm = pl.BlockSpec(memory_space=pl.ANY)
     piece = (2 * row_dev, half)
+    rest = 2 * cols // 7 // 256 * 256
+    wide = cols - rest
     scratch = [pltpu.VMEM(a.shape, a.dtype) for a in (
         queries, key_lift, value_lift, page_table, lengths, tree_parents, gain, expert_ids, route_weights
     )] + [
@@ -467,11 +512,16 @@
         pltpu.VMEM((nctx, half_rows, cols), F32),
         pltpu.VMEM((nctx, half_rows, cols), BF16),
         pltpu.VMEM((nctx, half_rows, cols), BF16),
-        pltpu.VMEM((nctx, half_rows, cols), BF16),
-        pltpu.VMEM((nctx, half_rows, cols), BF16),
-        pltpu.VMEM((nz,) + piece, F32),
-        pltpu.VMEM((nz,) + piece, BF16),
-        pltpu.VMEM((nz,) + piece, BF16),
+        pltpu.VMEM((nctx, half_rows, wide), BF16),
+        pltpu.VMEM((nctx, half_rows, wide), BF16),
+        pltpu.VMEM((nz, 2 * row_dev, wide // 2), F32),
+        pltpu.VMEM((nz, 2 * row_dev, wide // 2), BF16),
+        pltpu.VMEM((nz, 2 * row_dev, wide // 2), BF16),
+        pltpu.VMEM((nctx // 2, nz, 2 * row_dev, rest), F32),
+        pltpu.VMEM((nctx // 2, nz, 2 * row_dev, rest), BF16),
+        pltpu.VMEM((nctx // 2, nz, 2 * row_dev, rest), BF16),
+        pltpu.VMEM((nctx, 2 * row_dev, rest // 2), BF16),
+        pltpu.VMEM((nctx, 2 * row_dev, rest // 2), BF16),
         dma((15,)),
         dma((2 * nctx,)), dma((2 * nctx,)),
         dma, dma,
@@ -484,6 +534,8 @@
         dma((nctx,)), dma((nctx,)),
         dma((nctx,)), dma((nctx,)),
         dma((nz,)), dma((nz,)),
+        dma((nctx // 2, nz)), dma((nctx // 2, nz)),
+        dma((nctx,)), dma((nctx,)),
     ]
     return pl.pallas_call(
         functools.partial(kernel, nctx, nexp, page_pool.shape[1], own_leaves),

time: 43.3 us -> 41.6 us (0.961)
  Pallas kernels: 41.7 us -> 39.9 us
    pallas_call x1, Pallas kernels: 41.7 us -> 39.9 us  [local(): pl.pallas_call(functools.partial(kernel, nctx, nexp, page_pool.shape[1],...]
where the time goes in v1:
time: 41.6 us; the launch traced here: 41.3 us
  Pallas kernels  39.9 us (96%)
  local copies, waits for them, and re-layouts  1.36 us (3%)
    pallas_call x1, Pallas kernels, local(): pl.pallas_call(functools.partial(kernel, nctx, nexp, page_pool.shape[1],...  39.9 us
    unnamed x1, local copies, waits for them, and re-layouts  1.36 us

profile of v1, /device:TPU:0, one launch (start us, length us, event | category | flops | bytes accessed | tf_op | source)
XLA Modules:
  0.0 41.3 jit_solution(14286414361456014186)
XLA Ops:
  0.0 39.9 %shard_map.154 = bf16[8,1792]{1,0:T(8,128)(2,1)} custom-call(bf16[64,384]{1,0:T(8,128)(2,1)} %q_hbm.1, bf16[2,128,512]{2,1,0:T(8,128)(2,1)} %kl_hbm.1, bf16[2,512,128]{2,1,0:T(8,128)(2,1)} %vl_hbm.1, bf16[256,576]{1,0:T(8,128)(2,1)} %bitcast.10, bf16[16,576]{1,0:T(8,128)(2,1)} %bitcast.12, s32[8,12]{1,0:T(8,128)} %pt_hbm.1, s32[1,8]{1,0:T(1,128)} %bitcast.13, ...), custom_call_target="tpu_custom_call" | custom-call | tf_op jit(solution)/shard_map/pallas_call | solution.py:540
  39.9 1.4 %copy.18 = bf16[8,1792]{1,0:T(8,128)(2,1)} copy(bf16[8,1792]{1,0:T(8,128)(2,1)} %shard_map.154) | data formatting | bytes 57344
